TPU v7x, 32 devices: a whole 2x2x4 slice. The times are simulated.
32 devices in a mesh: expert: 8 (over z, x), wshard: 4 (over y, core).
Axes of the slice: x: 2, y: 2, z: 4, core: 2. Of those that a mesh axis runs over, the one named last changes fastest.
Arguments:
- images: bfloat16 [12608, 512], P(('expert', 'wshard')), may hold values from -6 to 6
- attn_in: bfloat16 [2, 512, 1536], P(None, 'wshard'), may hold values from -0.25 to 0.25
- attn_out: bfloat16 [2, 512, 512], P(None, 'wshard'), may hold values from -0.75 to 0.75
- norm_gains: bfloat16 [4, 512], P(None, 'wshard'), may hold values from 0.5 to 1.5
- mlp_in: bfloat16 [512, 2048], P('wshard'), may hold values from -0.25 to 0.25
- mlp_out: bfloat16 [2048, 512], P('wshard'), may hold values from -0.1875 to 0.1875
- router: bfloat16 [512, 8], P('wshard'), may hold values from -0.1875 to 0.1875
- expert_in: bfloat16 [8, 512, 2048], P('expert'), may hold values from -0.25 to 0.25
- expert_out: bfloat16 [8, 2048, 512], P('expert'), may hold values from -0.25 to 0.25
- expert_ids: int32 [12608, 2], P(('expert', 'wshard')), may hold values from 0 to 7, all different within a row; in each aligned block of 394 rows (0 to 393, 394 to 787, ...) at most 197 rows name the same one
- cotangent: bfloat16 [12608, 512], P(('expert', 'wshard')), may hold values from -6 to 6
Outputs:
- final: bfloat16 [12608, 512], P(('expert', 'wshard'))
- images_grad: float32 [12608, 512], P(('expert', 'wshard'))
- attn_in_grad: float32 [2, 512, 1536], P(None, 'wshard')
- attn_out_grad: float32 [2, 512, 512], P(None, 'wshard')
- norm_gains_grad: float32 [4, 512], P(None, 'wshard')
- mlp_in_grad: float32 [512, 2048], P('wshard')
- mlp_out_grad: float32 [2048, 512], P('wshard')
- router_grad: float32 [512, 8], P('wshard')
- expert_in_grad: float32 [8, 512, 2048], P('expert')
- expert_out_grad: float32 [8, 2048, 512], P('expert')
Inputs may be any that keep to these rules, and one draw needn't show every extreme that they name: `expert_ids`: each token names 2 different experts. The rows of one device name no expert more than 197 times, and in some device's rows one expert is named exactly 197 times.
All inputs are finite; a program needn't handle non-finite values.
Results may differ from a plain program's by a relative error of at most 0.023.
Values may be sent and summed in bfloat16 or wider, within the bound.
No kernel may reach another device: no remote copies, remote signals or barrier semaphores. Data moves between devices by JAX's collectives and lax.ppermute only.
A program may use at most 192 MiB of HBM per device.

v0:
```python
import jax
import jax.numpy as jnp
from jax import lax
from jax.sharding import PartitionSpec as P

D = 512
HEADS = 8
FF = 2048
SEQ = 197
TOP = 2


EPSILON = 1e-06


def normalize(layer_in, norm_gain):
    centred = layer_in - jnp.mean(layer_in, axis=-1, keepdims=True)
    spread = jnp.mean(centred * centred, axis=-1, keepdims=True)
    return centred * lax.rsqrt(spread + EPSILON) * norm_gain


def split_heads(packed):
    pictures = packed.shape[0] // SEQ
    shaped = packed.reshape(pictures, SEQ, 3, HEADS, packed.shape[1] // (3 * HEADS))
    return (shaped[:, :, 0], shaped[:, :, 1], shaped[:, :, 2])


def score_rows(queries, key_rows):
    factor = queries.shape[-1] ** (-0.5)
    return (
        jnp.einsum("gqhd,gkhd->ghqk", queries, key_rows, preferred_element_type=jnp.float32)
        * factor
    )


def attend_forward(layer_in, norm_gain, w_in, w_out):
    normed = normalize(layer_in, norm_gain).astype(jnp.bfloat16)
    packed = jnp.dot(normed, w_in, preferred_element_type=jnp.float32).astype(jnp.bfloat16)
    queries, key_rows, values = split_heads(packed)
    scores = score_rows(queries, key_rows)
    peak = jnp.max(scores, axis=-1, keepdims=True)
    raised = jnp.exp(scores - peak)
    summed = jnp.sum(raised, axis=-1, keepdims=True)
    chances = (raised / summed).astype(jnp.bfloat16)
    attended = jnp.einsum("ghqk,gkhd->gqhd", chances, values, preferred_element_type=jnp.float32)
    attended = attended.astype(jnp.bfloat16).reshape(layer_in.shape[0], -1)
    branch_out = jnp.dot(attended, w_out, preferred_element_type=jnp.float32)
    return (layer_in + branch_out, (packed, peak + jnp.log(summed), attended))


def attend_backward(layer_in, norm_gain, w_in, w_out, saved, grad_rows):
    packed, log_total, attended = saved
    grad_branch = grad_rows.astype(jnp.bfloat16)
    grad_w_out = jnp.einsum("td,te->de", attended, grad_branch, preferred_element_type=jnp.float32)
    grad_att = jnp.einsum(
        "te,de->td", grad_branch, w_out, preferred_element_type=jnp.float32
    ).astype(jnp.bfloat16)
    queries, key_rows, values = split_heads(packed)
    grad_att = grad_att.reshape(queries.shape)
    chances = jnp.exp(score_rows(queries, key_rows) - log_total)
    grad_chance = jnp.einsum(
        "gqhd,gkhd->ghqk", grad_att, values, preferred_element_type=jnp.float32
    )
    grad_values = jnp.einsum(
        "ghqk,gqhd->gkhd",
        chances.astype(jnp.bfloat16),
        grad_att,
        preferred_element_type=jnp.float32,
    )
    grad_scores = chances * (grad_chance - jnp.sum(grad_chance * chances, axis=-1, keepdims=True))
    grad_scores = grad_scores.astype(jnp.bfloat16)
    factor = queries.shape[-1] ** (-0.5)
    grad_queries = (
        jnp.einsum("ghqk,gkhd->gqhd", grad_scores, key_rows, preferred_element_type=jnp.float32)
        * factor
    )
    grad_keys = (
        jnp.einsum("ghqk,gqhd->gkhd", grad_scores, queries, preferred_element_type=jnp.float32)
        * factor
    )
    grad_packed = (
        jnp.stack([grad_queries, grad_keys, grad_values], axis=2)
        .reshape(packed.shape)
        .astype(jnp.bfloat16)
    )
    normed, norm_back = jax.vjp(normalize, layer_in, norm_gain)
    grad_w_in = jnp.einsum(
        "td,te->de", normed.astype(jnp.bfloat16), grad_packed, preferred_element_type=jnp.float32
    )
    grad_normed = jnp.einsum("te,de->td", grad_packed, w_in, preferred_element_type=jnp.float32)
    grad_input, grad_gain = norm_back(grad_normed)
    return (grad_rows + grad_input, grad_gain, grad_w_in, grad_w_out)


def feed_forward(layer_in, norm_gain, w_in, w_out):
    normed = normalize(layer_in, norm_gain).astype(jnp.bfloat16)
    hidden = jnp.dot(normed, w_in, preferred_element_type=jnp.float32)
    active = jax.nn.gelu(hidden).astype(jnp.bfloat16)
    return (layer_in + jnp.dot(active, w_out, preferred_element_type=jnp.float32), hidden)


def feed_backward(layer_in, norm_gain, w_in, w_out, hidden, grad_rows):
    grad_branch = grad_rows.astype(jnp.bfloat16)
    active, gelu_back = jax.vjp(jax.nn.gelu, hidden)
    grad_w_out = jnp.einsum(
        "tf,td->fd", active.astype(jnp.bfloat16), grad_branch, preferred_element_type=jnp.float32
    )
    grad_active = jnp.einsum("td,fd->tf", grad_branch, w_out, preferred_element_type=jnp.float32)
    grad_hidden = gelu_back(grad_active)[0].astype(jnp.bfloat16)
    normed, norm_back = jax.vjp(normalize, layer_in, norm_gain)
    grad_w_in = jnp.einsum(
        "td,tf->df", normed.astype(jnp.bfloat16), grad_hidden, preferred_element_type=jnp.float32
    )
    grad_normed = jnp.einsum("tf,df->td", grad_hidden, w_in, preferred_element_type=jnp.float32)
    grad_input, grad_gain = norm_back(grad_normed)
    return (grad_rows + grad_input, grad_gain, grad_w_in, grad_w_out)


def mixing_weights(logits, chosen):
    chances = jax.nn.softmax(logits, axis=-1)
    selector = (
        chosen[:, :, None] == jnp.arange(logits.shape[1], dtype=jnp.int32)[None, None, :]
    ).astype(jnp.float32)
    picked = jnp.sum(chances[:, None, :] * selector, axis=-1)
    return picked / jnp.sum(picked, axis=1, keepdims=True)


def local(
    images,
    attn_in,
    attn_out,
    norm_gains,
    mlp_in,
    mlp_out,
    router,
    expert_in,
    expert_out,
    expert_ids,
    cotangent,
):
    owners = lax.axis_size("expert")
    local_count = expert_in.shape[0]
    experts = owners * local_count
    tokens = images.shape[0]
    capacity = max(2, 2 * TOP * tokens // experts)
    gathered = (
        lax.all_gather(attn_in, "wshard", axis=1, tiled=True),
        lax.all_gather(attn_out, "wshard", axis=1, tiled=True),
        lax.all_gather(norm_gains, "wshard", axis=1, tiled=True),
        lax.all_gather(mlp_in, "wshard", axis=0, tiled=True),
        lax.all_gather(mlp_out, "wshard", axis=0, tiled=True),
        lax.all_gather(router, "wshard", axis=0, tiled=True),
    )
    full_attn_in, full_attn_out, gain_rows, full_mlp_in, full_mlp_out, full_router = gathered
    gain_rows = gain_rows.astype(jnp.float32)
    input_rows = images.astype(jnp.float32)
    after_first, saved_first = attend_forward(
        input_rows, gain_rows[0], full_attn_in[0], full_attn_out[0]
    )
    after_mlp, saved_hidden = feed_forward(after_first, gain_rows[1], full_mlp_in, full_mlp_out)
    after_second, saved_second = attend_forward(
        after_mlp, gain_rows[2], full_attn_in[1], full_attn_out[1]
    )
    routed_in = normalize(after_second, gain_rows[3]).astype(jnp.bfloat16)
    logits = jnp.dot(routed_in, full_router, preferred_element_type=jnp.float32)
    mixing = mixing_weights(logits, expert_ids)
    routed_ids = expert_ids.reshape(-1)
    matches = (routed_ids[:, None] == jnp.arange(experts, dtype=jnp.int32)[None, :]).astype(
        jnp.int32
    )
    slot_index = jnp.sum((jnp.cumsum(matches, axis=0) - 1) * matches, axis=1)
    outgoing = (
        jnp.zeros((experts, capacity, D), jnp.bfloat16)
        .at[routed_ids, slot_index]
        .set(jnp.repeat(routed_in, TOP, axis=0))
    )
    received = lax.all_to_all(outgoing, "expert", split_axis=0, concat_axis=0, tiled=True)
    slots = received.shape[1]
    grouped = received.reshape(owners, local_count, slots, D)
    hidden = jnp.einsum("nlcd,ldf->nlcf", grouped, expert_in, preferred_element_type=jnp.float32)
    active = jax.nn.gelu(hidden).astype(jnp.bfloat16)
    result = jnp.einsum("nlcf,lfd->nlcd", active, expert_out, preferred_element_type=jnp.float32)
    result = result.astype(jnp.bfloat16).reshape(experts, slots, D)
    returned = lax.all_to_all(result, "expert", split_axis=0, concat_axis=0, tiled=True)
    returned, arrived, expert_hidden = (returned, received, hidden.reshape(experts, slots, FF))
    expert_rows = returned[routed_ids, slot_index].astype(jnp.float32).reshape(tokens, TOP, D)
    final_rows = after_second + jnp.sum(mixing[:, :, None] * expert_rows, axis=1)
    regathered = (
        lax.all_gather(attn_in, "wshard", axis=1, tiled=True),
        lax.all_gather(attn_out, "wshard", axis=1, tiled=True),
        lax.all_gather(norm_gains, "wshard", axis=1, tiled=True),
        lax.all_gather(mlp_in, "wshard", axis=0, tiled=True),
        lax.all_gather(mlp_out, "wshard", axis=0, tiled=True),
        lax.all_gather(router, "wshard", axis=0, tiled=True),
    )
    full_attn_in, full_attn_out, gain_rows, full_mlp_in, full_mlp_out, full_router = regathered
    gain_rows = gain_rows.astype(jnp.float32)
    grad_final = cotangent.astype(jnp.float32)
    grad_mixing = jnp.sum(expert_rows * grad_final[:, None, :], axis=-1)
    grad_expert_rows = (
        (mixing[:, :, None] * grad_final[:, None, :]).astype(jnp.bfloat16).reshape(tokens * TOP, D)
    )
    grad_outgoing = (
        jnp.zeros((experts, capacity, D), jnp.bfloat16)
        .at[routed_ids, slot_index]
        .set(grad_expert_rows)
    )
    grad_arrived = lax.all_to_all(grad_outgoing, "expert", split_axis=0, concat_axis=0, tiled=True)
    grad_grouped = grad_arrived.reshape(owners, local_count, capacity, D)
    hidden_grouped = expert_hidden.reshape(owners, local_count, capacity, FF)
    active, gelu_back = jax.vjp(jax.nn.gelu, hidden_grouped)
    grad_expert_out = jnp.einsum(
        "nlcf,nlcd->lfd",
        active.astype(jnp.bfloat16),
        grad_grouped,
        preferred_element_type=jnp.float32,
    )
    grad_active = jnp.einsum(
        "nlcd,lfd->nlcf", grad_grouped, expert_out, preferred_element_type=jnp.float32
    )
    grad_hidden = gelu_back(grad_active)[0].astype(jnp.bfloat16)
    arrived_grouped = arrived.reshape(owners, local_count, capacity, D)
    grad_expert_in = jnp.einsum(
        "nlcd,nlcf->ldf", arrived_grouped, grad_hidden, preferred_element_type=jnp.float32
    )
    grad_sent = jnp.einsum(
        "nlcf,ldf->nlcd", grad_hidden, expert_in, preferred_element_type=jnp.float32
    )
    grad_sent = grad_sent.astype(jnp.bfloat16).reshape(experts, capacity, D)
    grad_back = lax.all_to_all(grad_sent, "expert", split_axis=0, concat_axis=0, tiled=True)
    grad_routed = jnp.sum(
        grad_back[routed_ids, slot_index].astype(jnp.float32).reshape(tokens, TOP, D), axis=1
    )
    mixing_back = jax.vjp(lambda values: mixing_weights(values, expert_ids), logits)[1]
    grad_logits = mixing_back(grad_mixing)[0].astype(jnp.bfloat16)
    grad_router = jnp.einsum(
        "td,te->de", routed_in, grad_logits, preferred_element_type=jnp.float32
    )
    grad_normed = grad_routed + jnp.einsum(
        "te,de->td", grad_logits, full_router, preferred_element_type=jnp.float32
    )
    norm_back = jax.vjp(normalize, after_second, gain_rows[3])[1]
    grad_input, gain_last = norm_back(grad_normed)
    grad_second = grad_final + grad_input
    grad_mlp_rows, gain_second, in_second, out_second = attend_backward(
        after_mlp, gain_rows[2], full_attn_in[1], full_attn_out[1], saved_second, grad_second
    )
    grad_first_rows, gain_mlp, mlp_in_grad, mlp_out_grad = feed_backward(
        after_first, gain_rows[1], full_mlp_in, full_mlp_out, saved_hidden, grad_mlp_rows
    )
    images_grad, gain_first, in_first, out_first = attend_backward(
        input_rows, gain_rows[0], full_attn_in[0], full_attn_out[0], saved_first, grad_first_rows
    )
    shares = (
        lax.psum_scatter(
            jnp.stack([in_first, in_second]).astype(jnp.bfloat16),
            "wshard",
            scatter_dimension=1,
            tiled=True,
        ).astype(jnp.float32),
        lax.psum_scatter(
            jnp.stack([out_first, out_second]).astype(jnp.bfloat16),
            "wshard",
            scatter_dimension=1,
            tiled=True,
        ).astype(jnp.float32),
        lax.psum_scatter(
            jnp.stack([gain_first, gain_mlp, gain_second, gain_last]).astype(jnp.bfloat16),
            "wshard",
            scatter_dimension=1,
            tiled=True,
        ).astype(jnp.float32),
        lax.psum_scatter(
            mlp_in_grad.astype(jnp.bfloat16), "wshard", scatter_dimension=0, tiled=True
        ).astype(jnp.float32),
        lax.psum_scatter(
            mlp_out_grad.astype(jnp.bfloat16), "wshard", scatter_dimension=0, tiled=True
        ).astype(jnp.float32),
        lax.psum_scatter(
            grad_router.astype(jnp.bfloat16), "wshard", scatter_dimension=0, tiled=True
        ).astype(jnp.float32),
    )
    totals = lax.psum((shares[0], shares[1], shares[2], shares[3], shares[4], shares[5]), "expert")
    expert_totals = (
        lax.psum(grad_expert_in.astype(jnp.bfloat16), "wshard").astype(jnp.float32),
        lax.psum(grad_expert_out.astype(jnp.bfloat16), "wshard").astype(jnp.float32),
    )
    return (
        final_rows.astype(jnp.bfloat16),
        images_grad,
        totals[0],
        totals[1],
        totals[2],
        totals[3],
        totals[4],
        totals[5],
        expert_totals[0],
        expert_totals[1],
    )


def solution(mesh):
    return jax.shard_map(
        local,
        mesh=mesh,
        in_specs=(
            P(("expert", "wshard"), None),
            P(None, "wshard", None),
            P(None, "wshard", None),
            P(None, "wshard"),
            P("wshard", None),
            P("wshard", None),
            P("wshard", None),
            P("expert", None, None),
            P("expert", None, None),
            P(("expert", "wshard"), None),
            P(("expert", "wshard"), None),
        ),
        out_specs=(
            P(("expert", "wshard"), None),
            P(("expert", "wshard"), None),
            P(None, "wshard", None),
            P(None, "wshard", None),
            P(None, "wshard"),
            P("wshard", None),
            P("wshard", None),
            P("wshard", None),
            P("expert", None, None),
            P("expert", None, None),
        ),
        check_vma=False,
    )
```

profile of v0, /device:TPU:0, one launch (start us, length us, event | category | flops | bytes accessed | tf_op | source)
XLA Modules:
  0.0 931.0 jit_solution(15635097109264904137)
XLA Ops:
  13.2 6.0 all_gather.24
  21.8 19.0 %all-gather.5.cloned.1.call-done = bf16[2,512,1536]{2,1,0:T(8,128)(2,1)} async-done(((bf16[2,128,1536]{2,1,0:T(8,128)(2,1)}), bf16[2,512,1536]{2,1,0:T(8,128)(2,1)}) %all-gather.5.cloned.1.call-update) | async-done | bytes 3145744 | tf_op jit(solution)/shard_map/all_gather | solution.py:147
  64.1 19.3 %all-gather.9.cloned.1.call-done = bf16[512,2048]{1,0:T(8,128)(2,1)} async-done(((bf16[128,2048]{1,0:T(8,128)(2,1)}), bf16[512,2048]{1,0:T(8,128)(2,1)}) %all-gather.9.cloned.1.call-update) | async-done | bytes 2097168 | tf_op jit(solution)/shard_map/all_gather | solution.py:150
  87.8 19.7 %all-gather.11.cloned.1.call-done = bf16[2048,512]{1,0:T(8,128)(2,1)} async-done(((bf16[512,512]{1,0:T(8,128)(2,1)}), bf16[2048,512]{1,0:T(8,128)(2,1)}) %all-gather.11.cloned.1.call-update) | async-done | bytes 2097168 | tf_op jit(solution)/shard_map/all_gather | solution.py:151
  136.2 105.0 %scatter_fusion = bf16[8,197,512]{2,0,1:T(8,128)(2,1)} fusion(bf16[8,197,512]{2,0,1:T(8,128)(2,1)} %broadcast.281.clone, s32[788]{0:T(1024)S(1)} %get-tuple-element.23, bf16[788,512]{1,0:T(8,128)(2,1)} %reshape.400), kind=kCustom, calls=%fused_computation.2 | custom fusion | bytes 2427040 | tf_op jit(solution)/shard_map/scatter | solution.py:175
  244.3 5.4 all-to-all-start
  265.2 105.0 %scatter_fusion.1 = bf16[8,197,512]{2,0,1:T(8,128)(2,1)} fusion(bf16[8,197,512]{2,0,1:T(8,128)(2,1)} %broadcast.281.clone.1, s32[788]{0:T(1024)S(1)} %get-tuple-element.23, bf16[788,512]{1,0:T(8,128)(2,1)} %multiply_convert_fusion.3), kind=kCustom, calls=%fused_computation.3 | custom fusion | bytes 2427040 | tf_op jit(solution)/shard_map/scatter | solution.py:206
  373.2 6.2 all-to-all-start.2
  379.4 5.7 fusion.45
  389.8 5.6 fusion.49
  395.4 23.0 %all-to-all-done.2 = bf16[8,197,512]{2,1,0:T(8,128)(2,1)} async-done(((bf16[8,197,512]{2,1,0:T(8,128)(2,1)}), bf16[8,197,512]{2,1,0:T(8,128)(2,1)}, u32[]{:S(2)}, u32[]{:S(2)}) %all-to-all-start.2) | async-done | bytes 1613856 | tf_op jit(solution)/shard_map/all_to_all | solution.py:208
  422.7 14.2 %fusion.6 = bf16[8,1,197,2048]{3,2,0,1:T(8,128)(2,1)S(1)} fusion(f32[8,197,2048]{2,1,0:T(8,128)} %copy-done.67, bf16[8,197,512]{2,1,0:T(8,128)(2,1)} %all-to-all-done.2, bf16[1,2048,512]{2,1,0:T(8,128)(2,1)S(1)} %copy-done), kind=kOutput, calls=%fused_computation.12 | convolution fusion | flops 3369664512 | bytes 23076864 | tf_op jit(solution)/shard_map/nlcd,lfd->nlcf/dot_general | solution.py:218
  442.1 6.7 fusion.34
  448.8 11.9 %all-to-all-done.1 = bf16[8,197,512]{2,1,0:T(8,128)(2,1)} async-done(((bf16[8,197,512]{2,1,0:T(8,128)(2,1)}), bf16[8,197,512]{2,1,0:T(8,128)(2,1)}, u32[]{:S(2)}, u32[]{:S(2)}) %all-to-all-start.1) | async-done | bytes 1613856 | tf_op jit(solution)/shard_map/all_to_all | solution.py:184
  465.1 10.1 %fusion.37 = bf16[1,2048,512]{2,1,0:T(8,128)(2,1)} fusion(bf16[8,197,512]{2,1,0:T(8,128)(2,1)} %all-to-all-done.2, f32[8,197,2048]{2,1,0:T(8,128)} %copy-done.67), kind=kOutput, calls=%fused_computation.64 | convolution fusion | flops 3335208960 | bytes 16621568 | tf_op jit(solution)/shard_map/nlcf,nlcd->lfd/dot_general | solution.py:212
  477.2 12.4 %gather_fusion = bf16[788,512]{1,0:T(8,128)(2,1)} fusion(bf16[8,197,512]{2,0,1:T(8,128)(2,1)S(1)} %copy.173, s32[788]{0:T(1024)S(1)} %get-tuple-element.22), kind=kCustom, calls=%fused_computation | custom fusion | bytes 1620128 | tf_op jit(solution)/shard_map/gather | solution.py:186
  491.8 5.9 multiply_reduce_fusion.4
  505.0 12.4 %gather_fusion.1 = bf16[788,512]{1,0:T(8,128)(2,1)} fusion(bf16[8,197,512]{2,0,1:T(8,128)(2,1)S(1)} %copy.176, s32[788]{0:T(1024)S(1)} %get-tuple-element.22), kind=kCustom, calls=%fused_computation.1 | custom fusion | bytes 1620128 | tf_op jit(solution)/shard_map/gather | solution.py:232
  606.4 11.3 %reduce-scatter.21.cloned.1.call-done = bf16[128,8]{1,0:T(8,128)(2,1)} async-done(((bf16[512,8]{1,0:T(8,128)(2,1)}), bf16[128,8]{1,0:T(8,128)(2,1)}) %reduce-scatter.21.cloned.1.call-update) | async-done | bytes 2064
  618.6 27.4 %reduce-scatter.13.cloned.1.call-done = bf16[2,128,512]{2,1,0:T(8,128)(2,1)} async-done(((bf16[2,512,512]{2,1,0:T(8,128)(2,1)}), bf16[2,128,512]{2,1,0:T(8,128)(2,1)}) %reduce-scatter.13.cloned.1.call-update) | async-done | bytes 262160 | tf_op jit(solution)/shard_map/reduce_scatter | solution.py:261
  645.9 34.0 %reduce-scatter.15.cloned.1.call-done = bf16[128,2048]{1,0:T(8,128)(2,1)} async-done(((bf16[512,2048]{1,0:T(8,128)(2,1)}), bf16[128,2048]{1,0:T(8,128)(2,1)}) %reduce-scatter.15.cloned.1.call-update) | async-done | bytes 524304 | tf_op jit(solution)/shard_map/reduce_scatter | solution.py:273
  679.9 34.0 %reduce-scatter.17.cloned.1.call-done = bf16[512,512]{1,0:T(8,128)(2,1)} async-done(((bf16[2048,512]{1,0:T(8,128)(2,1)}), bf16[512,512]{1,0:T(8,128)(2,1)}) %reduce-scatter.17.cloned.1.call-update) | async-done | bytes 524304 | tf_op jit(solution)/shard_map/reduce_scatter | solution.py:276
  713.9 40.5 %reduce-scatter.11.cloned.1.call-done = bf16[2,128,1536]{2,1,0:T(8,128)(2,1)} async-done(((bf16[2,512,1536]{2,1,0:T(8,128)(2,1)}), bf16[2,128,1536]{2,1,0:T(8,128)(2,1)}) %reduce-scatter.11.cloned.1.call-update) | async-done | bytes 786448 | tf_op jit(solution)/shard_map/reduce_scatter | solution.py:255
  754.4 169.8 %all-reduce.7 = (f32[2,128,1536]{2,1,0:T(8,128)}, f32[2,128,512]{2,1,0:T(8,128)}, f32[4,128]{1,0:T(4,128)}, f32[128,2048]{1,0:T(8,128)}, f32[512,512]{1,0:T(8,128)}, /*index=5*/f32[128,8]{0,1:T(8,128)}) all-reduce(bf16[2,128,1536]{2,1,0:T(8,128)(2,1)} %reduce-scatter.11.cloned.1.call-done, ...), channel_id=1, replica_groups=mesh['expert'=8,'wshard'=4] {'expert'}, use_global_device_ids=true, to_apply=%region_38.39 | all-reduce | flops 1050112 | bytes 6300672 | tf_op jit(solution)/shard_map/psum | solution.py:283
  (319 shorter events, 205.4 us)
Async XLA Ops:
  7.2 382.6 %copy-start = (bf16[1,2048,512]{2,1,0:T(8,128)(2,1)S(1)}, bf16[1,2048,512]{2,1,0:T(8,128)(2,1)}, u32[]{:S(2)}) copy-start(bf16[1,2048,512]{2,1,0:T(8,128)(2,1)} %param.19) | copy-start | bytes 6291460
  7.2 33.7 %all-gather.5.cloned.1.call-start = ((), (), s32[]{:S(2)}) async-start(), calls=%async_computation.10 | async-start | bytes 3932160 | tf_op jit(solution)/shard_map/all_gather | solution.py:147
  7.9 54.1 %all-gather.7.cloned.1.call-start = ((), (), s32[]{:S(2)}) async-start(), calls=%async_computation.11 | async-start | bytes 1310720 | tf_op jit(solution)/shard_map/all_gather | solution.py:148
  8.7 74.7 %all-gather.9.cloned.1.call-start = ((), (), s32[]{:S(2)}) async-start(), calls=%async_computation.12 | async-start | bytes 2621440 | tf_op jit(solution)/shard_map/all_gather | solution.py:150
  9.4 98.0 %all-gather.11.cloned.1.call-start = ((), (), s32[]{:S(2)}) async-start(), calls=%async_computation.13 | async-start | bytes 2621440 | tf_op jit(solution)/shard_map/all_gather | solution.py:151
  12.3 31.9 %copy-start.50 = (f32[394]{0:T(512)}, f32[394]{0:T(512)S(1)}, u32[]{:S(2)}) copy-start(f32[394]{0:T(512)S(1)} %broadcast_multiply_fusion.3) | copy-start | bytes 4732
  13.2 31.0 %copy-start.52 = (f32[394]{0:T(512)}, f32[394]{0:T(512)S(1)}, u32[]{:S(2)}) copy-start(f32[394]{0:T(512)S(1)} %fusion.128) | copy-start | bytes 4732
  19.2 25.0 %copy-start.54 = (f32[1,512]{1,0:T(1,128)}, f32[1,512]{1,0:T(1,128)S(1)}, u32[]{:S(2)}) copy-start(f32[1,512]{1,0:T(1,128)S(1)} %get-tuple-element.48) | copy-start | bytes 6148
  19.2 92.6 %copy-start.60 = (f32[1,512]{1,0:T(1,128)}, f32[1,512]{1,0:T(1,128)S(1)}, u32[]{:S(2)}) copy-start(f32[1,512]{1,0:T(1,128)S(1)} %get-tuple-element.46) | copy-start | bytes 6148
  63.8 43.6 %copy-start.15 = (f32[394,512]{1,0:T(8,128)}, f32[394,512]{1,0:T(8,128)S(1)}, u32[]{:S(2)}) copy-start(f32[394,512]{1,0:T(8,128)S(1)} %get-tuple-element.52) | copy-start | bytes 2420740
  244.3 128.9 %all-to-all-start = ((bf16[8,197,512]{2,1,0:T(8,128)(2,1)}), bf16[8,197,512]{2,1,0:T(8,128)(2,1)}, u32[]{:S(2)}, u32[]{:S(2)}) async-start(bf16[8,197,512]{2,1,0:T(8,128)(2,1)} %copy.172), calls=%async_computation | async-start | bytes 3276800 | tf_op jit(solution)/shard_map/all_to_all | solution.py:177
  249.7 11.3 %copy-start.49 = (s32[394,2]{0,1:T(2,128)S(1)}, s32[394,2]{0,1:T(2,128)}, u32[]{:S(2)}) copy-start(s32[394,2]{0,1:T(2,128)} %param.20) | copy-start | bytes 9460
  373.2 45.1 %all-to-all-start.2 = ((bf16[8,197,512]{2,1,0:T(8,128)(2,1)}), bf16[8,197,512]{2,1,0:T(8,128)(2,1)}, u32[]{:S(2)}, u32[]{:S(2)}) async-start(bf16[8,197,512]{2,1,0:T(8,128)(2,1)} %copy.175), calls=%async_computation.2 | async-start | bytes 3276800 | tf_op jit(solution)/shard_map/all_to_all | solution.py:208
  418.3 42.4 %all-to-all-start.1 = ((bf16[8,197,512]{2,1,0:T(8,128)(2,1)}), bf16[8,197,512]{2,1,0:T(8,128)(2,1)}, u32[]{:S(2)}, u32[]{:S(2)}) async-start(bf16[8,197,512]{2,1,0:T(8,128)(2,1)} %fusion.49), calls=%async_computation.1 | async-start | bytes 3276800 | tf_op jit(solution)/shard_map/all_to_all | solution.py:184
  422.6 14.2 %copy-start.65 = (bf16[1,512,2048]{2,1,0:T(8,128)(2,1)S(1)}, bf16[1,512,2048]{2,1,0:T(8,128)(2,1)}, u32[]{:S(2)}) copy-start(bf16[1,512,2048]{2,1,0:T(8,128)(2,1)} %param.18) | copy-start | bytes 6291460
  460.7 42.3 %all-to-all-start.3 = ((bf16[8,197,512]{2,1,0:T(8,128)(2,1)}), bf16[8,197,512]{2,1,0:T(8,128)(2,1)}, u32[]{:S(2)}, u32[]{:S(2)}) async-start(bf16[8,197,512]{2,1,0:T(8,128)(2,1)} %fusion.54), calls=%async_computation.3 | async-start | bytes 3276800 | tf_op jit(solution)/shard_map/all_to_all | solution.py:230
  465.0 132.4 %all-reduce.6.cloned.1.call-start = ((), (), s32[]{:S(2)}) async-start(), calls=%async_computation.20 | async-start | bytes 8388608 | tf_op jit(solution)/shard_map/psum | solution.py:285
  475.2 130.4 %reduce-scatter.19.cloned.1.call-start = ((), (), s32[]{:S(2)}) async-start(), calls=%async_computation.18 | async-start | bytes 163840
  577.3 40.5 %reduce-scatter.21.cloned.1.call-start = ((), (), s32[]{:S(2)}) async-start(), calls=%async_computation.19 | async-start | bytes 163840
  579.9 66.0 %reduce-scatter.13.cloned.1.call-start = ((), (), s32[]{:S(2)}) async-start(), calls=%async_computation.15 | async-start | bytes 1310720 | tf_op jit(solution)/shard_map/reduce_scatter | solution.py:261
  582.1 97.9 %reduce-scatter.15.cloned.1.call-start = ((), (), s32[]{:S(2)}) async-start(), calls=%async_computation.16 | async-start | bytes 2621440 | tf_op jit(solution)/shard_map/reduce_scatter | solution.py:273
  586.5 127.4 %reduce-scatter.17.cloned.1.call-start = ((), (), s32[]{:S(2)}) async-start(), calls=%async_computation.17 | async-start | bytes 2621440 | tf_op jit(solution)/shard_map/reduce_scatter | solution.py:276
  591.3 163.1 %reduce-scatter.11.cloned.1.call-start = ((), (), s32[]{:S(2)}) async-start(), calls=%async_computation.14 | async-start | bytes 3932160 | tf_op jit(solution)/shard_map/reduce_scatter | solution.py:255
  601.8 322.5 %copy-start.1 = (bf16[1,2048,512]{2,1,0:T(8,128)(2,1)S(1)}, bf16[1,2048,512]{2,1,0:T(8,128)(2,1)}, u32[]{:S(2)}) copy-start(bf16[1,2048,512]{2,1,0:T(8,128)(2,1)} %param.19) | copy-start | bytes 6291460
  (60 other events, 211.0 us)
Sparse Core Ops, SparseCore 0:
  9.6 31.2 all-gather.4
  42.4 16.7 all-gather.6
  60.8 22.5 all-gather.8
  84.8 22.5 all-gather.10
  475.3 86.0 all-reduce.5
  577.4 17.7 reduce-scatter.18
  598.1 19.5 reduce-scatter.20
  621.0 24.8 reduce-scatter.12
  648.5 31.4 reduce-scatter.14
  682.5 31.3 reduce-scatter.16
  716.5 37.9 reduce-scatter.10
where the time goes:
time: 943 us; the launch traced here: 931 us
  local copies, waits for them, and re-layouts  320 us (34%)
  waiting for transfers between devices  248 us (26%)
  blocking collectives  181 us (19%)
  matrix products  108 us (11%)
  other arithmetic  37.6 us (4%)
  starting transfers between devices  20.9 us (2%)
  between operations  15.4 us (2%)
    psum x1, blocking collectives, local(): lax.psum((shares[0], shares[1], shares[2], shares[3], shares[4], shares[5...  170 us
    scatter x2, local copies, waits for them, and re-layouts, local(): outgoing = jnp.zeros((experts, capacity, D), jnp.bfloat16).at[routed_ids,...  108 us
    scatter x2, local copies, waits for them, and re-layouts, local(): grad_outgoing = jnp.zeros((experts, capacity, D), jnp.bfloat16).at[routed...  108 us
    reduce_scatter x1, waiting for transfers between devices, local(): lax.psum_scatter(jnp.stack([in_first, in_second]).astype(jnp.bfloat16), '...  40.5 us
    reduce_scatter x1, waiting for transfers between devices, local(): lax.psum_scatter(mlp_in_grad.astype(jnp.bfloat16), 'wshard', scatter_dime...  34 us
    reduce_scatter x1, waiting for transfers between devices, local(): lax.psum_scatter(mlp_out_grad.astype(jnp.bfloat16), 'wshard', scatter_dim...  34 us
    reduce_scatter x1, waiting for transfers between devices, local(): lax.psum_scatter(jnp.stack([out_first, out_second]).astype(jnp.bfloat16),...  27.4 us
    unnamed x149, local copies, waits for them, and re-layouts  25.4 us
  transfers between devices with their start and end apart: 15, of which 11 were waited for; matrix products, arithmetic and copies ran while one was open for 34% of the time, Pallas kernels for 0%

commit v1 on v0

v1 whole, which is shorter than its diff:
```python
import functools

import jax
import jax.numpy as jnp
from jax import lax
from jax.experimental import pallas as pl
from jax.experimental.pallas import tpu as pltpu
from jax.sharding import PartitionSpec as P

D = 512
HEADS = 8
FF = 2048
SEQ = 197
TOP = 2
HEAD_DIM = 64
PAD = 208
EXTRA = 16
CHUNK = 512
EPSILON = 1e-06
ROOT_2_PI = 0.7978845608028654
CUBIC = 0.044715

F32 = jnp.float32
BF16 = jnp.bfloat16
VMEM_LIMIT = 56 * 1024 * 1024


def dot(a, b, ca=1, cb=0):
    return lax.dot_general(a, b, (((ca,), (cb,)), ((), ())), preferred_element_type=F32)


def unit_rows(rows):
    centred = rows - jnp.mean(rows, axis=-1, keepdims=True)
    scale = lax.rsqrt(jnp.mean(centred * centred, axis=-1, keepdims=True) + EPSILON)
    return centred * scale, scale


def norm_backward(unit, scale, gain, grad):
    scaled = gain * grad
    inner = (
        scaled
        - jnp.mean(scaled, axis=-1, keepdims=True)
        - unit * jnp.mean(scaled * unit, axis=-1, keepdims=True)
    )
    return inner * scale, jnp.sum(grad * unit, axis=0, keepdims=True)


def gelu_parts(h):
    square = h * h
    t = jnp.tanh(ROOT_2_PI * h * (1.0 + CUBIC * square))
    half = 0.5 * (1.0 + t)
    slope = half + 0.5 * h * (1.0 - t * t) * (ROOT_2_PI * (1.0 + 3.0 * CUBIC * square))
    return h * half, slope


def gelu(h):
    return 0.5 * h * (1.0 + jnp.tanh(ROOT_2_PI * h * (1.0 + CUBIC * h * h)))


def start_weight(pos_ref, pieces, held, sems, first):
    copies = []
    for j, piece in enumerate(pieces):
        copy = pltpu.make_async_copy(piece, held.at[pos_ref[0] ^ j], sems.at[first + j])
        copy.start()
        copies.append(copy)
    return copies


def wait_all(copies):
    for copy in copies:
        copy.wait()


def softmax_rows(q, k):
    scores = dot(q, k, 1, 1) * (HEAD_DIM**-0.5)
    column = lax.broadcasted_iota(jnp.int32, scores.shape, 1)
    scores = jnp.where(column < SEQ, scores, -1e30)
    raised = jnp.exp(scores - jnp.max(scores, axis=-1, keepdims=True))
    return raised * (1.0 / jnp.sum(raised, axis=-1, keepdims=True))


def attend_forward_kernel(pos_ref, x_ref, gain_ref, *refs):
    wi, wo = refs[0:4], refs[4:8]
    y_ref, packed_ref, o_ref, wi_held, wo_held, sems = refs[8:]
    wi_copies = start_weight(pos_ref, wi, wi_held, sems, 0)
    wo_copies = start_weight(pos_ref, wo, wo_held, sems, 4)
    rows = x_ref[...].astype(F32)
    unit, _ = unit_rows(rows)
    normed = (unit * gain_ref[...]).astype(BF16)
    wait_all(wi_copies)
    packed_ref[...] = dot(normed, wi_held[...].reshape(D, 3 * D)).astype(BF16)
    lane = lax.broadcasted_iota(jnp.int32, (PAD, 2 * HEAD_DIM), 1)
    for image in range(x_ref.shape[0] // PAD):
        here = pl.ds(image * PAD, PAD)
        for pair in range(HEADS // 2):
            at = pair * 2 * HEAD_DIM
            q = packed_ref[here, at : at + 128]
            k = packed_ref[here, D + at : D + at + 128]
            v = packed_ref[here, 2 * D + at : 2 * D + at + 128]
            total = None
            for side in range(2):
                mine = (lane >= HEAD_DIM) == bool(side)
                chances = softmax_rows(jnp.where(mine, q, jnp.zeros_like(q)), k).astype(BF16)
                part = dot(chances, jnp.where(mine, v, jnp.zeros_like(v)))
                total = part if total is None else total + part
            o_ref[here, at : at + 128] = total.astype(BF16)
    wait_all(wo_copies)
    y_ref[...] = x_ref[...].astype(F32) + dot(o_ref[...], wo_held[...].reshape(D, D))


def attend_backward_kernel(smalls, pos_ref, x_ref, gain_ref, packed_ref, o_ref, dz_ref, *refs):
    wi, wo = refs[0:4], refs[4:8]
    extra = refs[8 : 8 + smalls]
    dx_ref, dgain_ref, send_ref, keep_ref, wi_held, wo_held, dp_ref, dout_ref, do_ref, normed_ref, sems = refs[
        8 + smalls :
    ]
    wo_copies = start_weight(pos_ref, wo, wo_held, sems, 4)
    wi_copies = start_weight(pos_ref, wi, wi_held, sems, 0)
    unit, scale = unit_rows(x_ref[...].astype(F32))
    gain = gain_ref[...]
    normed_ref[...] = (unit * gain).astype(BF16)
    dout_ref[...] = dz_ref[...].astype(BF16)
    wait_all(wo_copies)
    do_ref[...] = dot(dout_ref[...], wo_held[...].reshape(D, D), 1, 1).astype(BF16)
    lane = lax.broadcasted_iota(jnp.int32, (PAD, 2 * HEAD_DIM), 1)
    factor = HEAD_DIM**-0.5
    for image in range(x_ref.shape[0] // PAD):
        here = pl.ds(image * PAD, PAD)
        for pair in range(HEADS // 2):
            at = pair * 2 * HEAD_DIM
            q = packed_ref[here, at : at + 128]
            k = packed_ref[here, D + at : D + at + 128]
            v = packed_ref[here, 2 * D + at : 2 * D + at + 128]
            do = do_ref[here, at : at + 128]
            dq = dk = dv = None
            for side in range(2):
                mine = (lane >= HEAD_DIM) == bool(side)
                own = lambda a: jnp.where(mine, a, jnp.zeros_like(a))
                q_own, k_own, do_own = own(q), own(k), own(do)
                chances = softmax_rows(q_own, k)
                dv_part = dot(chances.astype(BF16), do_own, 0, 0)
                da = dot(do_own, v, 1, 1)
                ds = chances * (da - jnp.sum(da * chances, axis=-1, keepdims=True))
                ds = ds.astype(BF16)
                dq_part = dot(ds, k_own)
                dk_part = dot(ds, q_own, 0, 0)
                dq = dq_part if dq is None else dq + dq_part
                dk = dk_part if dk is None else dk + dk_part
                dv = dv_part if dv is None else dv + dv_part
            dp_ref[here, at : at + 128] = (dq * factor).astype(BF16)
            dp_ref[here, D + at : D + at + 128] = (dk * factor).astype(BF16)
            dp_ref[here, 2 * D + at : 2 * D + at + 128] = dv.astype(BF16)
    wait_all(wi_copies)
    dn = dot(dp_ref[...], wi_held[...].reshape(D, 3 * D), 1, 1)
    unit, scale = unit_rows(x_ref[...].astype(F32))
    dx, dgain = norm_backward(unit, scale, gain, dn)
    dx_ref[...] = dz_ref[...] + dx
    dgain_ref[...] = dgain
    for target, flip in ((send_ref, 1), (keep_ref, 0)):
        for place in range(2):
            shard = pos_ref[0] ^ (flip + 2 * (1 - place))
            columns = pl.ds(pl.multiple_of(shard * 128, 128), 128)
            target[place, 0:128, 0 : 3 * D] = dot(normed_ref[:, columns], dp_ref[...], 0, 0).astype(BF16)
            target[place, 0:128, 3 * D : 4 * D] = dot(o_ref[:, columns], dout_ref[...], 0, 0).astype(BF16)
    if smalls:
        small = jnp.concatenate([dgain] + [ref[...] for ref in extra], axis=0)
        small = jnp.concatenate([small, jnp.zeros((EXTRA - small.shape[0] % EXTRA, D), F32)], axis=0)
        for target, flip in ((send_ref, 1), (keep_ref, 0)):
            for place in range(2):
                shard = pos_ref[0] ^ (flip + 2 * (1 - place))
                piece = jnp.zeros((small.shape[0], 128), F32)
                for s in range(4):
                    piece = jnp.where(shard == s, small[:, s * 128 : (s + 1) * 128], piece)
                target[place, 128:, 0:128] = piece.astype(BF16)
                target[place, 128:, 128:] = jnp.zeros((small.shape[0], 4 * D - 128), BF16)


def feed_forward_kernel(pos_ref, x_ref, gain_ref, *refs):
    w1, w2 = refs[0:4], refs[4:8]
    y_ref, w1_held, w2_held, sems = refs[8:]
    w1_copies = start_weight(pos_ref, w1, w1_held, sems, 0)
    w2_copies = start_weight(pos_ref, w2, w2_held, sems, 4)
    unit, _ = unit_rows(x_ref[...])
    normed = (unit * gain_ref[...]).astype(BF16)
    wait_all(w1_copies)
    total = x_ref[...]
    for j in range(FF // CHUNK):
        at = slice(j * CHUNK, (j + 1) * CHUNK)
        active = gelu(dot(normed, w1_held[:, :, at].reshape(D, CHUNK))).astype(BF16)
        if j == 0:
            wait_all(w2_copies)
        total = total + dot(active, w2_held[...].reshape(FF, D)[at])
    y_ref[...] = total


def feed_backward_kernel(pos_ref, x_ref, gain_ref, dz_ref, *refs):
    w1, w2 = refs[0:4], refs[4:8]
    dx_ref, dgain_ref, send1_ref, keep1_ref, send2_ref, keep2_ref, w1_held, w2_held, g1_ref, g2_ref, sems = refs[8:]
    w1_copies = start_weight(pos_ref, w1, w1_held, sems, 0)
    w2_copies = start_weight(pos_ref, w2, w2_held, sems, 4)
    unit, scale = unit_rows(x_ref[...])
    gain = gain_ref[...]
    normed = (unit * gain).astype(BF16)
    dout = dz_ref[...].astype(BF16)
    wait_all(w1_copies)
    wait_all(w2_copies)
    dn = None
    for j in range(FF // CHUNK):
        at = slice(j * CHUNK, (j + 1) * CHUNK)
        w1_now = w1_held[:, :, at].reshape(D, CHUNK)
        w2_now = w2_held[...].reshape(FF, D)[at]
        active, slope = gelu_parts(dot(normed, w1_now))
        dh = (slope * dot(dout, w2_now, 1, 1)).astype(BF16)
        g2_ref[at] = dot(active.astype(BF16), dout, 0, 0).astype(BF16)
        g1_ref[:, at] = dot(normed, dh, 0, 0).astype(BF16)
        part = dot(dh, w1_now, 1, 1)
        dn = part if dn is None else dn + part
    dx, dgain = norm_backward(unit, scale, gain, dn)
    dx_ref[...] = dz_ref[...] + dx
    dgain_ref[...] = dgain
    for one, two, flip in ((send1_ref, send2_ref, 1), (keep1_ref, keep2_ref, 0)):
        for place in range(2):
            shard = pos_ref[0] ^ (flip + 2 * (1 - place))
            one[place] = g1_ref[pl.ds(pl.multiple_of(shard * 128, 128), 128)]
            two[place] = g2_ref[pl.ds(pl.multiple_of(shard * 512, 512), 512)]


def routing_kernel(slots, ids_ref, cot_ref, index_ref, blocks_ref):
    experts = blocks_ref.shape[0] // slots
    tokens = ids_ref.shape[1]
    expert = lax.broadcasted_iota(jnp.int32, (experts, tokens), 0)
    named = [ids_ref[k : k + 1, :] == expert for k in range(TOP)]
    matches = jnp.where(named[0] | named[1], 1.0, 0.0).astype(BF16)
    earlier = lax.broadcasted_iota(jnp.int32, (tokens, tokens), 0) < lax.broadcasted_iota(
        jnp.int32, (tokens, tokens), 1
    )
    rank = dot(matches, jnp.where(earlier, 1.0, 0.0).astype(BF16))
    index_ref[...] = jnp.full(index_ref.shape, -1, jnp.int32)
    place = lax.broadcasted_iota(jnp.int32, (blocks_ref.shape[0], tokens), 0)
    chosen = None
    for k in range(TOP):
        slot = jnp.sum(jnp.where(named[k], rank, 0.0), axis=0, keepdims=True).astype(jnp.int32)
        index = ids_ref[k : k + 1, :] * slots + slot
        index_ref[k : k + 1, :] = index
        hit = place == index
        chosen = hit if chosen is None else chosen | hit
    blocks_ref[...] = dot(jnp.where(chosen, 1.0, 0.0).astype(BF16), cot_ref[...]).astype(BF16)


def write_spare(target, block, slots, column):
    eye = lax.broadcasted_iota(jnp.int32, (slots, D), 0) == lax.broadcasted_iota(jnp.int32, (slots, D), 1)
    line = jnp.sum(jnp.where(eye, column, 0.0), axis=0, keepdims=True)
    high = line.astype(BF16).astype(F32)
    middle = (line - high).astype(BF16).astype(F32)
    low = line - high - middle
    row = lax.broadcasted_iota(jnp.int32, (8, D), 0)
    return jnp.where(row == 0, high, jnp.where(row == 1, middle, jnp.where(row == 2, low, 0.0)))


def read_spare(tile, slots):
    line = tile[0:1] + tile[1:2] + tile[2:3]
    eye = lax.broadcasted_iota(jnp.int32, (slots, D), 0) == lax.broadcasted_iota(jnp.int32, (slots, D), 1)
    return jnp.sum(jnp.where(eye, line, 0.0), axis=1, keepdims=True)


def dispatch_kernel(slots, x_ref, gain_ref, router_ref, ids_ref, index_ref, c_ref, gate_ref, blocks_ref):
    experts = blocks_ref.shape[0] // slots
    tokens = x_ref.shape[0]
    unit, _ = unit_rows(x_ref[...])
    c = (unit * gain_ref[...]).astype(BF16)
    c_ref[...] = c
    logits = dot(router_ref[...], c, 1, 1)
    expert = lax.broadcasted_iota(jnp.int32, (experts, tokens), 0)
    picked = [
        jnp.sum(jnp.where(ids_ref[k : k + 1, :] == expert, logits, 0.0), axis=0, keepdims=True) for k in range(TOP)
    ]
    gates = [0.5 + 0.5 * jnp.tanh(0.5 * (picked[k] - picked[1 - k])) for k in range(TOP)]
    gate_ref[...] = jnp.concatenate(gates + [jnp.zeros((8 - TOP, tokens), F32)], axis=0)
    for e in range(experts):
        place = lax.broadcasted_iota(jnp.int32, (slots, tokens), 0) + e * slots
        hits = [place == index_ref[k : k + 1, :] for k in range(TOP)]
        rows = dot(jnp.where(hits[0] | hits[1], 1.0, 0.0).astype(BF16), c)
        weight = sum(jnp.where(hits[k], gates[k], 0.0) for k in range(TOP))
        tile = write_spare(None, None, slots, jnp.sum(weight, axis=1, keepdims=True))
        blocks_ref[e * slots : (e + 1) * slots] = jnp.concatenate([rows[: slots - 8], tile], axis=0).astype(BF16)


def experts_kernel(c_ref, g_ref, w1_ref, w2_ref, dc_ref, z_ref, dw1_ref, dw2_ref, acc1, acc2):
    together, slots, _ = c_ref.shape
    step = pl.program_id(0)

    @pl.when(step == 0)
    def _():
        acc1[...] = jnp.zeros_like(acc1)
        acc2[...] = jnp.zeros_like(acc2)

    rows = together * slots
    gate = jnp.concatenate([read_spare(c_ref[b, slots - 8 :].astype(F32), slots) for b in range(together)], axis=0)
    c = c_ref[...].reshape(rows, D)
    g = g_ref[...].reshape(rows, D).astype(F32)
    dy = (gate * g).astype(BF16)
    y = dc = None
    for j in range(FF // CHUNK):
        at = slice(j * CHUNK, (j + 1) * CHUNK)
        active, slope = gelu_parts(dot(c, w1_ref[:, at]))
        active = active.astype(BF16)
        dh = (slope * dot(dy, w2_ref[at], 1, 1)).astype(BF16)
        y_part = dot(active, w2_ref[at])
        dc_part = dot(dh, w1_ref[:, at], 1, 1)
        y = y_part if y is None else y + y_part
        dc = dc_part if dc is None else dc + dc_part
        acc1[:, at] += dot(c, dh, 0, 0)
        acc2[at] += dot(active, dy, 0, 0)
    y = y.astype(BF16).astype(F32)
    dgate = jnp.sum(g * y, axis=1, keepdims=True)
    z_ref[...] = (gate * y).astype(BF16).reshape(together, slots, D)
    for b in range(together):
        here = slice(b * slots, (b + 1) * slots)
        tile = write_spare(None, None, slots, dgate[here])
        dc_ref[b] = jnp.concatenate([dc[here][: slots - 8], tile], axis=0).astype(BF16)

    @pl.when(step == pl.num_programs(0) - 1)
    def _():
        dw1_ref[...] = acc1[...].astype(BF16)
        dw2_ref[...] = acc2[...].astype(BF16)


def one_hot_columns(index_ref, width):
    place = lax.broadcasted_iota(jnp.int32, (index_ref.shape[0], width), 1)
    hit = (place == index_ref[:, 0:1]) | (place == index_ref[:, 1:2])
    return jnp.where(hit, 1.0, 0.0).astype(BF16)


def combine_kernel(
    slots, blocks_ref, x_ref, gain_ref, router_ref, ids_ref, index_ref, turned_ref, c_ref, gate_ref, cot_ref,
    dx_ref, dgain_ref, drouter_ref,
):
    experts = blocks_ref.shape[0] // slots
    tokens = x_ref.shape[0]
    gc = dot(one_hot_columns(turned_ref, blocks_ref.shape[0]), blocks_ref[...])
    dgates = [jnp.zeros((1, tokens), F32) for _ in range(TOP)]
    for e in range(experts):
        place = lax.broadcasted_iota(jnp.int32, (slots, tokens), 0) + e * slots
        column = read_spare(blocks_ref[(e + 1) * slots - 8 : (e + 1) * slots].astype(F32), slots)
        for k in range(TOP):
            hit = place == index_ref[k : k + 1, :]
            dgates[k] = dgates[k] + jnp.sum(jnp.where(hit, column, 0.0), axis=0, keepdims=True)
    dl = gate_ref[0:1] * gate_ref[1:2] * (dgates[0] - dgates[1])
    expert = lax.broadcasted_iota(jnp.int32, (experts, tokens), 0)
    dlogits = jnp.where(ids_ref[0:1, :] == expert, dl, 0.0) - jnp.where(ids_ref[1:2, :] == expert, dl, 0.0)
    dlogits = dlogits.astype(BF16)
    gc = gc + dot(dlogits, router_ref[...], 0, 0)
    drouter_ref[...] = dot(dlogits, c_ref[...])
    unit, scale = unit_rows(x_ref[...])
    dx, dgain = norm_backward(unit, scale, gain_ref[...], gc)
    dx_ref[...] = cot_ref[...].astype(F32) + dx
    dgain_ref[...] = dgain


def final_kernel(blocks_ref, x_ref, turned_ref, out_ref):
    out_ref[...] = (x_ref[...] + dot(one_hot_columns(turned_ref, blocks_ref.shape[0]), blocks_ref[...])).astype(BF16)


def call(kernel, outs, *args, scratch=(), specs=None, **more):
    return pl.pallas_call(
        kernel,
        out_shape=[jax.ShapeDtypeStruct(shape, kind) for shape, kind in outs],
        in_specs=specs if specs is not None else [pl.BlockSpec(memory_space=pltpu.VMEM)] * len(args),
        out_specs=[pl.BlockSpec(memory_space=pltpu.VMEM)] * len(outs),
        scratch_shapes=list(scratch),
        compiler_params=pltpu.CompilerParams(vmem_limit_bytes=VMEM_LIMIT),
        **more,
    )(*args)


WHOLE = pl.BlockSpec(memory_space=pltpu.VMEM)
SCALAR = pl.BlockSpec(memory_space=pltpu.SMEM)
AWAY = pl.BlockSpec(memory_space=pl.ANY)


def flip(array, axis, bit):
    return lax.ppermute(array, axis, [(i, i ^ bit) for i in range(lax.axis_size(axis))])


def gather_pieces(piece):
    across = flip(piece, "wshard", 2)
    return (piece, flip(piece, "wshard", 1), across, flip(across, "wshard", 1))


def sum_over_wshard(send, keep):
    half = (keep.astype(F32) + flip(send, "wshard", 1).astype(F32)).astype(BF16)
    return (half[1].astype(F32) + flip(half[0], "wshard", 2).astype(F32)).astype(BF16)


def sum_over_expert(shard):
    owners = lax.axis_size("expert")
    parts = shard.reshape(owners, -1, shard.shape[-1] if shard.shape[0] % owners == 0 else 128)
    parts = lax.all_to_all(parts, "expert", split_axis=0, concat_axis=0, tiled=True)
    own = jnp.sum(parts.astype(F32), axis=0, keepdims=True).astype(BF16)
    every = lax.all_to_all(
        jnp.broadcast_to(own, (owners,) + own.shape[1:]), "expert", split_axis=0, concat_axis=0, tiled=True
    )
    return every.reshape(shard.shape)


def expand(rows, images):
    return jnp.pad(rows.reshape(images, SEQ, -1), ((0, 0), (0, PAD - SEQ), (0, 0))).reshape(images * PAD, -1)


def contract(rows, images):
    return rows.reshape(images, PAD, -1)[:, :SEQ].reshape(images * SEQ, -1)


def local(
    images, attn_in, attn_out, norm_gains, mlp_in, mlp_out, router, expert_in, expert_out, expert_ids, cotangent
):
    owners = lax.axis_size("expert")
    experts = owners * expert_in.shape[0]
    tokens = images.shape[0]
    pictures = tokens // SEQ
    rows = pictures * PAD
    capacity = max(2, 2 * TOP * tokens // experts)
    slots = (capacity + 8 + 15) // 16 * 16
    every = experts * slots
    pos = lax.axis_index("wshard").astype(jnp.int32).reshape(1)

    small = jnp.concatenate([norm_gains, router.T], axis=0)
    small = jnp.pad(small, ((0, -small.shape[0] % 16), (0, 0)))
    small_pieces = gather_pieces(small)
    small_full = jnp.zeros((4,) + small.shape, BF16)
    for j, piece in enumerate(small_pieces):
        small_full = lax.dynamic_update_slice(small_full, piece[None], (pos[0] ^ j, 0, 0))
    small_full = small_full.transpose(1, 0, 2).reshape(small.shape[0], D)
    gains = [small_full[i : i + 1].astype(F32) for i in range(4)]
    router_full = small_full[4 : 4 + experts]

    wi = [gather_pieces(attn_in[0]), None]
    wo = [gather_pieces(attn_out[0]), None]
    w1 = gather_pieces(mlp_in)
    w2 = gather_pieces(mlp_out)
    wi[1] = gather_pieces(attn_in[1])
    wo[1] = gather_pieces(attn_out[1])

    ids = jnp.pad(expert_ids.T.reshape(TOP, pictures, SEQ), ((0, 8 - TOP), (0, 0), (0, PAD - SEQ)), constant_values=-1)
    ids = ids.reshape(8, rows)
    cot = expand(cotangent, pictures)
    x0 = expand(images, pictures)

    index, g_out = call(
        functools.partial(routing_kernel, slots), [((8, rows), jnp.int32), ((every, D), BF16)], ids, cot
    )
    turned = index.T
    trade = functools.partial(lax.all_to_all, axis_name="expert", split_axis=0, concat_axis=0, tiled=True)
    g_in = trade(g_out.reshape(experts, slots, D))

    weight_specs = [AWAY] * 8
    attn_scratch = [pltpu.VMEM((4, D // 4, 3 * D), BF16), pltpu.VMEM((4, D // 4, D), BF16)]
    mlp_scratch = [pltpu.VMEM((4, D // 4, FF), BF16), pltpu.VMEM((4, FF // 4, D), BF16)]
    sems = pltpu.SemaphoreType.DMA((8,))

    def attend(x, layer):
        return call(
            attend_forward_kernel,
            [((rows, D), F32), ((rows, 3 * D), BF16), ((rows, D), BF16)],
            pos, x, gains[2 * layer], *wi[layer], *wo[layer],
            specs=[SCALAR, WHOLE, WHOLE] + weight_specs,
            scratch=attn_scratch + [sems],
        )

    def attend_back(x, layer, packed, o, dz, extra):
        tall = 128 + (EXTRA if extra else 0) * ((sum(a.shape[0] for a in extra) + 1 + EXTRA - 1) // EXTRA)
        return call(
            functools.partial(attend_backward_kernel, len(extra)),
            [((rows, D), F32), ((1, D), F32), ((2, tall, 4 * D), BF16), ((2, tall, 4 * D), BF16)],
            pos, x, gains[2 * layer], packed, o, dz, *wi[layer], *wo[layer], *extra,
            specs=[SCALAR] + [WHOLE] * 5 + weight_specs + [WHOLE] * len(extra),
            scratch=attn_scratch
            + [pltpu.VMEM((rows, 3 * D), BF16)]
            + [pltpu.VMEM((rows, D), BF16)] * 3
            + [sems],
        )

    x1, packed1, o1 = attend(x0, 0)
    (x2,) = call(
        feed_forward_kernel, [((rows, D), F32)], pos, x1, gains[1], *w1, *w2,
        specs=[SCALAR, WHOLE, WHOLE] + weight_specs, scratch=mlp_scratch + [sems],
    )
    x3, packed2, o2 = attend(x2, 1)
    c, gate, c_out = call(
        functools.partial(dispatch_kernel, slots),
        [((rows, D), BF16), ((8, rows), F32), ((every, D), BF16)],
        x3, gains[3], router_full, ids, index,
    )
    c_in = trade(c_out.reshape(experts, slots, D))

    together = 1
    while together * 2 * slots <= 512 and experts % (together * 2) == 0:
        together *= 2
    block = pl.BlockSpec((together, slots, D), lambda i: (i, 0, 0))
    fixed1 = pl.BlockSpec((D, FF), lambda i: (0, 0))
    fixed2 = pl.BlockSpec((FF, D), lambda i: (0, 0))
    dc_out, z_out, dw1, dw2 = pl.pallas_call(
        experts_kernel,
        grid=(experts // together,),
        in_specs=[block, block, fixed1, fixed2],
        out_specs=[block, block, fixed1, fixed2],
        out_shape=[
            jax.ShapeDtypeStruct((experts, slots, D), BF16),
            jax.ShapeDtypeStruct((experts, slots, D), BF16),
            jax.ShapeDtypeStruct((D, FF), BF16),
            jax.ShapeDtypeStruct((FF, D), BF16),
        ],
        scratch_shapes=[pltpu.VMEM((D, FF), F32), pltpu.VMEM((FF, D), F32)],
        compiler_params=pltpu.CompilerParams(vmem_limit_bytes=VMEM_LIMIT),
    )(c_in, g_in, expert_in[0], expert_out[0])
    dc_in = trade(dc_out)
    z_in = trade(z_out)

    g3, gain3, drouter = call(
        functools.partial(combine_kernel, slots),
        [((rows, D), F32), ((1, D), F32), ((experts, D), F32)],
        dc_in.reshape(every, D), x3, gains[3], router_full, ids, index, turned, c, gate, cot,
    )
    g2, gain2, send, keep = attend_back(x2, 1, packed2, o2, g3, [])
    second = sum_over_expert(sum_over_wshard(send, keep))
    g1, gain1, send1, keep1, send2, keep2 = call(
        feed_backward_kernel,
        [((rows, D), F32), ((1, D), F32)]
        + [((2, D // 4, FF), BF16)] * 2
        + [((2, FF // 4, D), BF16)] * 2,
        pos, x1, gains[1], g2, *w1, *w2,
        specs=[SCALAR, WHOLE, WHOLE, WHOLE] + weight_specs,
        scratch=mlp_scratch + [pltpu.VMEM((D, FF), BF16), pltpu.VMEM((FF, D), BF16), sems],
    )
    mlp1 = sum_over_expert(sum_over_wshard(send1, keep1))
    mlp2 = sum_over_expert(sum_over_wshard(send2, keep2))
    dx, _, send, keep = attend_back(x0, 0, packed1, o1, g1, [gain1, gain2, gain3, drouter])
    first = sum_over_expert(sum_over_wshard(send, keep))
    (final,) = call(final_kernel, [((rows, D), BF16)], z_in.reshape(every, D), x3, turned)

    def sum_experts(grad):
        half = grad.shape[0] // 2
        core = pos[0] % 2
        send = lax.dynamic_slice_in_dim(grad, (1 - core) * half, half)
        keep = lax.dynamic_slice_in_dim(grad, core * half, half)
        part = (keep.astype(F32) + flip(send, "wshard", 1).astype(F32)).astype(BF16)
        part = (part.astype(F32) + flip(part, "wshard", 2).astype(F32)).astype(BF16)
        other = flip(part, "wshard", 1)
        whole = jnp.where(core == 0, jnp.concatenate([part, other]), jnp.concatenate([other, part]))
        return whole.astype(F32)[None]

    small = first[128:, 0:128].astype(F32)
    return (
        contract(final, pictures),
        contract(dx, pictures),
        jnp.stack([first[:128, : 3 * D], second[:, : 3 * D]]).astype(F32),
        jnp.stack([first[:128, 3 * D :], second[:, 3 * D :]]).astype(F32),
        small[0:4],
        mlp1.astype(F32),
        mlp2.astype(F32),
        small[4 : 4 + experts].T,
        sum_experts(dw1),
        sum_experts(dw2),
    )


def solution(mesh):
    rows = P(("expert", "wshard"), None)
    dense = (P(None, "wshard", None), P(None, "wshard", None), P(None, "wshard"))
    shards = (P("wshard", None),) * 3
    experts = (P("expert", None, None),) * 2
    return jax.shard_map(
        local,
        mesh=mesh,
        in_specs=(rows, *dense, *shards, *experts, rows, rows),
        out_specs=(rows, rows, *dense, *shards, *experts),
        check_vma=False,
    )
```

time: 943 us -> 473 us (0.50)
  local copies, waits for them, and re-layouts: 320 us -> 38.1 us
  blocking collectives: 181 us -> 46.7 us
  matrix products: 108 us -> 0 us
  Pallas kernels: 0 us -> 108 us
  waiting for transfers between devices: 248 us -> 166 us
  starting transfers between devices: 20.9 us -> 70.4 us
  between operations: 15.4 us -> 1.54 us
    scatter x4 -> x0, local copies, waits for them, and re-layouts: 216 us -> none  [the longest x2 108 us: local(): outgoing = jnp.zeros((experts, capacity, D), jnp.bfloat16).at[routed_ids,...]
    psum x1 -> x0, blocking collectives: 170 us -> none  [local(): lax.psum((shares[0], shares[1], shares[2], shares[3], shares[4], shares[5...]
    reduce_scatter x4 -> x0, waiting for transfers between devices: 136 us -> none  [the longest x1 40.5 us: local(): lax.psum_scatter(jnp.stack([in_first, in_second]).astype(jnp.bfloat16), '...]
    pallas_call x0 -> x11, Pallas kernels: none -> 108 us  [the longest x10 74.9 us: call(): pl.pallas_call(kernel, out_shape=[jax.ShapeDtypeStruct(shape, kind) for s...]
    dot_general x39 -> x0, matrix products: 108 us -> none  [the longest x1 14.2 us: local(): jnp.einsum('nlcd,lfd->nlcf', grad_grouped, expert_out, preferred_element_...]
    all_to_all x4 -> x11, waiting for transfers between devices: 40 us -> 104 us  [the longest x1 38.4 us: local(): dc_in = trade(dc_out)]
    ppermute x0 -> x35, waiting for transfers between devices: none -> 62.6 us  [flip(): lax.ppermute(array, axis, [(i, i ^ bit) for i in range(lax.axis_size(axis...]
    all_gather x4 -> x0, waiting for transfers between devices: 58 us -> none  [the longest x1 19.7 us: local(): lax.all_gather(mlp_out, 'wshard', axis=0, tiled=True)]
  transfers between devices with their start and end apart: 15 -> 46, of which waited for: 11 -> 15; matrix products, arithmetic and copies ran while one was open for 34% -> 13% of each run, Pallas kernels for 0% -> 11%
where the time goes in v1:
time: 473 us; the launch traced here: 467 us
  waiting for transfers between devices  166 us (35%)
  Pallas kernels  108 us (23%)
  starting transfers between devices  70.4 us (15%)
  blocking collectives  46.7 us (10%)
  local copies, waits for them, and re-layouts  38.1 us (8%)
  other arithmetic  35.6 us (8%)
    pallas_call x10, Pallas kernels, call(): pl.pallas_call(kernel, out_shape=[jax.ShapeDtypeStruct(shape, kind) for s...  74.9 us
    ppermute x35, waiting for transfers between devices, flip(): lax.ppermute(array, axis, [(i, i ^ bit) for i in range(lax.axis_size(axis...  62.6 us
    all_to_all x1, blocking collectives, local(): c_in = trade(c_out.reshape(experts, slots, D))  46.7 us
    all_to_all x1, waiting for transfers between devices, local(): dc_in = trade(dc_out)  38.4 us
    all_to_all x4, waiting for transfers between devices, sum_over_expert(): lax.all_to_all(parts, 'expert', split_axis=0, concat_axis=0, tiled=True)  35.7 us
    pallas_call x1, Pallas kernels, local(): pl.pallas_call(experts_kernel, grid=(experts // together,), in_specs=[blo...  33.6 us
    all_to_all x4, waiting for transfers between devices, sum_over_expert(): lax.all_to_all(jnp.broadcast_to(own, (owners,) + own.shape[1:]), 'expert'...  29.4 us
    ppermute x35, starting transfers between devices, flip(): lax.ppermute(array, axis, [(i, i ^ bit) for i in range(lax.axis_size(axis...  19.6 us
  transfers between devices with their start and end apart: 46, of which 15 were waited for; matrix products, arithmetic and copies ran while one was open for 13% of the time, Pallas kernels for 11%

profile of v1, /device:TPU:0, one launch (start us, length us, event | category | flops | bytes accessed | tf_op | source)
XLA Modules:
  0.0 467.1 jit_solution(1585639462479733277)
XLA Ops:
  7.4 7.4 %all-to-all-start.1 = ((bf16[8,208,512]{2,1,0:T(8,128)(2,1)}), bf16[8,208,512]{2,1,0:T(8,128)(2,1)S(1)}, u32[]{:S(2)}, u32[]{:S(2)}) async-start(bf16[8,208,512]{2,1,0:T(8,128)(2,1)} %bitcast.101), calls=%async_computation.1 | async-start | bytes 3407872 | tf_op jit(solution)/shard_map/all_to_all | solution.py:454
  19.6 8.2 %collective-permute-done.1 = bf16[16,128]{1,0:T(8,128)(2,1)S(1)} collective-permute-done((bf16[16,128]{1,0:T(8,128)(2,1)S(1)}, bf16[16,128]{1,0:T(8,128)(2,1)S(1)}, u32[]{:S(2)}, u32[]{:S(2)}) %collective-permute-start.1) | collective-permute-done | bytes 4128 | tf_op jit(solution)/shard_map/ppermute | solution.py:382
  34.2 13.6 %collective-permute-done.19.refs_6_ = bf16[128,512]{1,0:T(8,128)(2,1)S(1)} collective-permute-done((bf16[128,512]{1,0:T(8,128)(2,1)S(1)}, bf16[128,512]{1,0:T(8,128)(2,1)S(1)}, u32[]{:S(2)}, u32[]{:S(2)}) %collective-permute-start.19) | collective-permute-done | bytes 131104 | tf_op jit(solution)/shard_map/ppermute | solution.py:382
  51.2 18.5 %collective-permute-done.16.refs_2_ = bf16[128,1536]{1,0:T(8,128)(2,1)S(1)} collective-permute-done((bf16[128,1536]{1,0:T(8,128)(2,1)S(1)}, bf16[128,1536]{1,0:T(8,128)(2,1)S(1)}, u32[]{:S(2)}, u32[]{:S(2)}) %collective-permute-start.16) | collective-permute-done | bytes 393248 | tf_op jit(solution)/shard_map/ppermute | solution.py:382
  84.0 6.8 %shard_map.186 = (f32[416,512]{1,0:T(8,128)}, bf16[416,1536]{1,0:T(8,128)(2,1)}, bf16[416,512]{1,0:T(8,128)(2,1)}) custom-call(s32[1]{0:T(128)} %bitcast.pos_ref, bf16[416,512]{1,0:T(8,128)(2,1)} %bitcast.95, f32[1,512]{1,0:T(1,128)} %bitcast.109, bf16[128,1536]{1,0:T(8,128)(2,1)} %copy-done.5, bf16[128,1536]{1,0:T(8,128)(2,1)} %copy-done.14, ...), custom_call_target="tpu_custom_call" | custom-call | tf_op jit(solution)/shard_map/pallas_call | solution.py:365
  90.8 6.4 %shard_map.187.x_ref = f32[416,512]{1,0:T(8,128)} custom-call(s32[1]{0:T(128)} %bitcast.pos_ref, f32[416,512]{1,0:T(8,128)} %get-tuple-element.41.x_ref, f32[1,512]{1,0:T(1,128)} %bitcast.111, bf16[128,2048]{1,0:T(8,128)(2,1)} %refs_0_.3, bf16[128,2048]{1,0:T(8,128)(2,1)} %collective-permute-done.9.refs_1_, ...), custom_call_target="tpu_custom_call" | custom-call | tf_op jit(solution)/shard_map/pallas_call | solution.py:365
  98.2 7.0 %shard_map.188 = (f32[416,512]{1,0:T(8,128)}, bf16[416,1536]{1,0:T(8,128)(2,1)}, bf16[416,512]{1,0:T(8,128)(2,1)}) custom-call(s32[1]{0:T(128)} %bitcast.pos_ref, f32[416,512]{1,0:T(8,128)} %shard_map.187.x_ref, f32[1,512]{1,0:T(1,128)} %bitcast.115, bf16[128,1536]{1,0:T(8,128)(2,1)} %copy-done.6, bf16[128,1536]{1,0:T(8,128)(2,1)} %copy-done.16, ...), custom_call_target="tpu_custom_call" | custom-call | tf_op jit(solution)/shard_map/pallas_call | solution.py:365
  109.8 46.7 %all_to_all.60.c_ref = bf16[8,208,512]{2,1,0:T(8,128)(2,1)} all-to-all(bf16[8,208,512]{2,1,0:T(8,128)(2,1)} %bitcast.102), channel_id=1, replica_groups=mesh['expert'=8,'wshard'=4] {'expert'}, dimensions={0} | all-to-all | bytes 3407872 | tf_op jit(solution)/shard_map/all_to_all | solution.py:494
  156.5 33.6 %shard_map.191 = (bf16[8,208,512]{2,1,0:T(8,128)(2,1)}, bf16[8,208,512]{2,1,0:T(8,128)(2,1)}, bf16[512,2048]{1,0:T(8,128)(2,1)}, bf16[2048,512]{1,0:T(8,128)(2,1)}) custom-call(bf16[8,208,512]{2,1,0:T(8,128)(2,1)} %all_to_all.60.c_ref, bf16[8,208,512]{2,1,0:T(8,128)(2,1)} %copy-done.2, bf16[512,2048]{1,0:T(8,128)(2,1)} %bitcast.97, bf16[2048,512]{1,0:T(8,128)(2,1)} %bitcast.98), custom_call_target="tpu_custom_call" | custom-call | tf_op jit(solution)/shard_map/pallas_call | solution.py:502
  195.0 38.4 %all-to-all-done.3 = bf16[8,208,512]{2,1,0:T(8,128)(2,1)S(1)} async-done(((bf16[8,208,512]{2,1,0:T(8,128)(2,1)}), bf16[8,208,512]{2,1,0:T(8,128)(2,1)S(1)}, u32[]{:S(2)}, u32[]{:S(2)}) %all-to-all-start.3) | async-done | bytes 1703968 | tf_op jit(solution)/shard_map/all_to_all | solution.py:516
  234.6 5.4 %shard_map.193 = (f32[416,512]{1,0:T(8,128)}, f32[1,512]{1,0:T(1,128)}, f32[8,512]{1,0:T(8,128)}) custom-call(bf16[1664,512]{1,0:T(8,128)(2,1)} %bitcast.90, f32[416,512]{1,0:T(8,128)} %get-tuple-element.42.x_ref, f32[1,512]{1,0:T(1,128)} %bitcast.114, bf16[8,512]{1,0:T(8,128)(2,1)} %bitcast.106, s32[8,416]{1,0:T(8,128)} %reshape.295.ids_ref, ...), custom_call_target="tpu_custom_call" | custom-call | tf_op jit(solution)/shard_map/pallas_call | solution.py:365
  240.0 12.4 %shard_map.194 = (f32[416,512]{1,0:T(8,128)}, f32[1,512]{1,0:T(1,128)}, bf16[2,128,2048]{2,1,0:T(8,128)(2,1)}, bf16[2,128,2048]{2,1,0:T(8,128)(2,1)}) custom-call(s32[1]{0:T(128)} %bitcast.pos_ref, f32[416,512]{1,0:T(8,128)} %shard_map.187.x_ref, f32[1,512]{1,0:T(1,128)} %bitcast.116, bf16[416,1536]{1,0:T(8,128)(2,1)} %get-tuple-element.49.packed_ref, ...), custom_call_target="tpu_custom_call" | custom-call | tf_op jit(solution)/shard_map/pallas_call | solution.py:365
  256.3 12.3 %shard_map.195 = (f32[416,512]{1,0:T(8,128)}, f32[1,512]{1,0:T(1,128)}, bf16[2,128,2048]{2,1,0:T(8,128)(2,1)}, bf16[2,128,2048]{2,1,0:T(8,128)(2,1)}, bf16[2,512...) custom-call(s32[1]{0:T(128)} %bitcast.pos_ref, f32[416,512]{1,0:T(8,128)} %get-tuple-element.41.x_ref, ...), custom_call_target="tpu_custom_call" | custom-call | tf_op jit(solution)/shard_map/pallas_call | solution.py:365
  270.2 13.1 %shard_map.196 = (f32[416,512]{1,0:T(8,128)}, f32[1,512]{1,0:T(1,128)}, bf16[2,144,2048]{2,1,0:T(8,128)(2,1)}, bf16[2,144,2048]{2,1,0:T(8,128)(2,1)}) custom-call(s32[1]{0:T(128)} %bitcast.pos_ref, bf16[416,512]{1,0:T(8,128)(2,1)} %bitcast.96, f32[1,512]{1,0:T(1,128)} %bitcast.110, bf16[416,1536]{1,0:T(8,128)(2,1)} %get-tuple-element.47.packed_ref, ...), custom_call_target="tpu_custom_call" | custom-call | tf_op jit(solution)/shard_map/pallas_call | solution.py:365
  287.9 11.2 %collective-permute-done.24 = bf16[128,2048]{1,0:T(8,128)(2,1)S(1)} collective-permute-done((bf16[128,2048]{1,0:T(8,128)(2,1)S(1)}, bf16[128,2048]{1,0:T(8,128)(2,1)S(1)}, u32[]{:S(2)}, u32[]{:S(2)}) %collective-permute-start.24) | collective-permute-done | bytes 524320 | tf_op jit(solution)/shard_map/ppermute | solution.py:382
  300.1 6.0 %all-to-all-start.6 = ((bf16[8,16,2048]{2,1,0:T(8,128)(2,1)}), bf16[8,16,2048]{2,1,0:T(8,128)(2,1)S(1)}, u32[]{:S(2)}, u32[]{:S(2)}) async-start(bf16[8,16,2048]{2,1,0:T(8,128)(2,1)} %bitcast.32), calls=%async_computation.6 | async-start | bytes 1048576 | tf_op jit(solution)/shard_map/all_to_all | solution.py:398
  312.6 6.6 %all-to-all-done.6 = bf16[8,16,2048]{2,1,0:T(8,128)(2,1)S(1)} async-done(((bf16[8,16,2048]{2,1,0:T(8,128)(2,1)}), bf16[8,16,2048]{2,1,0:T(8,128)(2,1)S(1)}, u32[]{:S(2)}, u32[]{:S(2)}) %all-to-all-start.6) | async-done | bytes 524320 | tf_op jit(solution)/shard_map/all_to_all | solution.py:398
  330.0 6.7 %all-to-all-done.8 = bf16[8,16,2048]{2,1,0:T(8,128)(2,1)} async-done(((bf16[8,16,2048]{2,1,0:T(8,128)(2,1)}), bf16[8,16,2048]{2,1,0:T(8,128)(2,1)}, u32[]{:S(2)}, u32[]{:S(2)}) %all-to-all-start.8) | async-done | bytes 524320 | tf_op jit(solution)/shard_map/all_to_all | solution.py:398
  344.2 10.0 %all-to-all-done.10 = bf16[8,64,512]{2,1,0:T(8,128)(2,1)} async-done(((bf16[8,64,512]{2,1,0:T(8,128)(2,1)}), bf16[8,64,512]{2,1,0:T(8,128)(2,1)}, u32[]{:S(2)}, u32[]{:S(2)}) %all-to-all-start.10) | async-done | bytes 524320 | tf_op jit(solution)/shard_map/all_to_all | solution.py:398
  365.0 12.4 %all-to-all-done.4 = bf16[8,18,2048]{2,1,0:T(8,128)(2,1)S(1)} async-done(((bf16[8,18,2048]{2,1,0:T(8,128)(2,1)}), bf16[8,18,2048]{2,1,0:T(8,128)(2,1)S(1)}, u32[]{:S(2)}, u32[]{:S(2)}) %all-to-all-start.4) | async-done | bytes 589856 | tf_op jit(solution)/shard_map/all_to_all | solution.py:398
  388.9 7.7 %all-to-all-done.7 = bf16[8,16,2048]{2,1,0:T(8,128)(2,1)} async-done(((bf16[8,16,2048]{2,1,0:T(8,128)(2,1)}), bf16[8,16,2048]{2,1,0:T(8,128)(2,1)}, u32[]{:S(2)}, u32[]{:S(2)}) %all-to-all-start.7) | async-done | bytes 524320 | tf_op jit(solution)/shard_map/all_to_all | solution.py:400
  401.7 4.7 %collective-permute-done.33 = bf16[1024,512]{1,0:T(8,128)(2,1)} collective-permute-done((bf16[1024,512]{1,0:T(8,128)(2,1)S(1)}, bf16[1024,512]{1,0:T(8,128)(2,1)}, u32[]{:S(2)}, u32[]{:S(2)}) %collective-permute-start.33) | collective-permute-done | bytes 1048608 | tf_op jit(solution)/shard_map/ppermute | solution.py:382
  417.5 5.7 %all-to-all-start.9 = ((bf16[8,16,2048]{2,1,0:T(8,128)(2,1)}), bf16[8,16,2048]{2,1,0:T(8,128)(2,1)S(1)}, u32[]{:S(2)}, u32[]{:S(2)}) async-start(bf16[8,16,2048]{2,1,0:T(8,128)(2,1)} %broadcast_in_dim.48), calls=%async_computation.9 | async-start | bytes 1048576 | tf_op jit(solution)/shard_map/all_to_all | solution.py:400
  446.0 17.3 %all-to-all-done.5 = bf16[8,18,2048]{2,1,0:T(8,128)(2,1)S(1)} async-done(((bf16[8,18,2048]{2,1,0:T(8,128)(2,1)}), bf16[8,18,2048]{2,1,0:T(8,128)(2,1)S(1)}, u32[]{:S(2)}, u32[]{:S(2)}) %all-to-all-start.5) | async-done | bytes 589856 | tf_op jit(solution)/shard_map/all_to_all | solution.py:400
  (214 shorter events, 147.3 us)
Async XLA Ops:
  7.4 102.4 %all-to-all-start.1 = ((bf16[8,208,512]{2,1,0:T(8,128)(2,1)}), bf16[8,208,512]{2,1,0:T(8,128)(2,1)S(1)}, u32[]{:S(2)}, u32[]{:S(2)}) async-start(bf16[8,208,512]{2,1,0:T(8,128)(2,1)} %bitcast.101), calls=%async_computation.1 | async-start | bytes 3407872 | tf_op jit(solution)/shard_map/all_to_all | solution.py:454
  16.0 34.5 %collective-permute-start.3 = (bf16[128,1536]{1,0:T(8,128)(2,1)S(1)}, bf16[128,1536]{1,0:T(8,128)(2,1)S(1)}, u32[]{:S(2)}, u32[]{:S(2)}) collective-permute-start(bf16[128,1536]{1,0:T(8,128)(2,1)S(1)} %get-tuple-element.73.refs_0_), channel_id=1, source_target_pairs={{0,1},{1,0},{2,3},{3,2},{4,5},{5,4},{6,7},{7,6},{8,9},{9,8},{10,11... | collective-permute-start | bytes 1179656 | tf_op jit(solution)/shard_map/ppermute | solution.py:382
  16.1 34.5 %collective-permute-start.4 = (bf16[128,1536]{1,0:T(8,128)(2,1)S(1)}, bf16[128,1536]{1,0:T(8,128)(2,1)}, u32[]{:S(2)}, u32[]{:S(2)}) collective-permute-start(bf16[128,1536]{1,0:T(8,128)(2,1)S(1)} %get-tuple-element.73.refs_0_), channel_id=1, source_target_pairs={{0,2},{1,3},{2,0},{3,1},{4,6},{5,7},{6,4},{7,5},{8,10},{9,11},{10,... | collective-permute-start | bytes 1179656 | tf_op jit(solution)/shard_map/ppermute | solution.py:382
  29.4 21.7 %collective-permute-start.10 = (bf16[128,2048]{1,0:T(8,128)(2,1)S(1)}, bf16[128,2048]{1,0:T(8,128)(2,1)}, u32[]{:S(2)}, u32[]{:S(2)}) collective-permute-start(bf16[128,2048]{1,0:T(8,128)(2,1)S(1)} %copy-done.12), channel_id=1, source_target_pairs={{0,2},{1,3},{2,0},{3,1},{4,6},{5,7},{6,4},{7,5},{8,10},{9,11},{10,... | collective-permute-start | bytes 1572872 | tf_op jit(solution)/shard_map/ppermute | solution.py:382
  47.7 21.9 %collective-permute-start.13 = (bf16[512,512]{1,0:T(8,128)(2,1)S(1)}, bf16[512,512]{1,0:T(8,128)(2,1)}, u32[]{:S(2)}, u32[]{:S(2)}) collective-permute-start(bf16[512,512]{1,0:T(8,128)(2,1)S(1)} %copy-done.13), channel_id=1, source_target_pairs={{0,2},{1,3},{2,0},{3,1},{4,6},{5,7},{6,4},{7,5},{8,10},{9,11},{10,... | collective-permute-start | bytes 1572872 | tf_op jit(solution)/shard_map/ppermute | solution.py:382
  49.9 19.7 %collective-permute-start.16 = (bf16[128,1536]{1,0:T(8,128)(2,1)S(1)}, bf16[128,1536]{1,0:T(8,128)(2,1)S(1)}, u32[]{:S(2)}, u32[]{:S(2)}) collective-permute-start(bf16[128,1536]{1,0:T(8,128)(2,1)S(1)} %get-tuple-element.72.refs_0_), channel_id=1, source_target_pairs={{0,2},{1,3},{2,0},{3,1},{4,6},{5,7},{6,4},{7,5},{8,10},{9,11},{10,... | collective-permute-start | bytes 1179656 | tf_op jit(solution)/shard_map/ppermute | solution.py:382
  50.6 31.1 %collective-permute-start.9 = (bf16[128,2048]{1,0:T(8,128)(2,1)S(1)}, bf16[128,2048]{1,0:T(8,128)(2,1)}, u32[]{:S(2)}, u32[]{:S(2)}) collective-permute-start(bf16[128,2048]{1,0:T(8,128)(2,1)S(1)} %copy-done.12), channel_id=1, source_target_pairs={{0,1},{1,0},{2,3},{3,2},{4,5},{5,4},{6,7},{7,6},{8,9},{9,8},{10,11... | collective-permute-start | bytes 1572872 | tf_op jit(solution)/shard_map/ppermute | solution.py:382
  50.6 31.1 %collective-permute-start.12 = (bf16[512,512]{1,0:T(8,128)(2,1)S(1)}, bf16[512,512]{1,0:T(8,128)(2,1)}, u32[]{:S(2)}, u32[]{:S(2)}) collective-permute-start(bf16[512,512]{1,0:T(8,128)(2,1)S(1)} %copy-done.13), channel_id=1, source_target_pairs={{0,1},{1,0},{2,3},{3,2},{4,5},{5,4},{6,7},{7,6},{8,9},{9,8},{10,11... | collective-permute-start | bytes 1572872 | tf_op jit(solution)/shard_map/ppermute | solution.py:382
  51.1 31.8 %collective-permute-start.11 = (bf16[128,2048]{1,0:T(8,128)(2,1)}, bf16[128,2048]{1,0:T(8,128)(2,1)}, u32[]{:S(2)}, u32[]{:S(2)}) collective-permute-start(bf16[128,2048]{1,0:T(8,128)(2,1)} %collective-permute-done.10.refs_2_), channel_id=1, source_target_pairs={{0,1},{1,0},{2,3},{3,2},{4,5},{5,4},{6,7},{7,6},{8,9},{9,8},{10,11... | collective-permute-start | bytes 1572872 | tf_op jit(solution)/shard_map/ppermute | solution.py:382
  69.7 21.1 %collective-permute-start.14 = (bf16[512,512]{1,0:T(8,128)(2,1)}, bf16[512,512]{1,0:T(8,128)(2,1)}, u32[]{:S(2)}, u32[]{:S(2)}) collective-permute-start(bf16[512,512]{1,0:T(8,128)(2,1)} %collective-permute-done.13.refs_6_), channel_id=1, source_target_pairs={{0,1},{1,0},{2,3},{3,2},{4,5},{5,4},{6,7},{7,6},{8,9},{9,8},{10,11... | collective-permute-start | bytes 1572872 | tf_op jit(solution)/shard_map/ppermute | solution.py:382
  190.2 43.3 %all-to-all-start.3 = ((bf16[8,208,512]{2,1,0:T(8,128)(2,1)}), bf16[8,208,512]{2,1,0:T(8,128)(2,1)S(1)}, u32[]{:S(2)}, u32[]{:S(2)}) async-start(bf16[8,208,512]{2,1,0:T(8,128)(2,1)} %get-tuple-element.51), calls=%async_computation.3 | async-start | bytes 3407872 | tf_op jit(solution)/shard_map/all_to_all | solution.py:516
  252.4 31.5 %collective-permute-start.23 = (bf16[2,128,2048]{2,1,0:T(8,128)(2,1)}, bf16[2,128,2048]{2,1,0:T(8,128)(2,1)S(1)}, u32[]{:S(2)}, u32[]{:S(2)}) collective-permute-start(bf16[2,128,2048]{2,1,0:T(8,128)(2,1)} %get-tuple-element.65), channel_id=1, source_target_pairs={{0,1},{1,0},{2,3},{3,2},{4,5},{5,4},{6,7},{7,6},{8,9},{9,8},{10,11... | collective-permute-start | bytes 3145736 | tf_op jit(solution)/shard_map/ppermute | solution.py:382
  252.5 47.6 %all-to-all-start.2 = ((bf16[8,208,512]{2,1,0:T(8,128)(2,1)}), bf16[8,208,512]{2,1,0:T(8,128)(2,1)S(1)}, u32[]{:S(2)}, u32[]{:S(2)}) async-start(bf16[8,208,512]{2,1,0:T(8,128)(2,1)} %get-tuple-element.46), calls=%async_computation.2 | async-start | bytes 3407872 | tf_op jit(solution)/shard_map/all_to_all | solution.py:517
  270.2 87.7 %collective-permute-start.29 = (bf16[256,2048]{1,0:T(8,128)(2,1)}, bf16[256,2048]{1,0:T(8,128)(2,1)}, u32[]{:S(2)}, u32[]{:S(2)}) collective-permute-start(bf16[256,2048]{1,0:T(8,128)(2,1)} %constant_dynamic-slice_fusion.1), channel_id=1, source_target_pairs={{0,1},{1,0},{2,3},{3,2},{4,5},{5,4},{6,7},{7,6},{8,9},{9,8},{10,11... | collective-permute-start | bytes 3145736 | tf_op jit(solution)/shard_map/ppermute | solution.py:382
  283.3 40.0 %collective-permute-start.21 = (bf16[2,144,2048]{2,1,0:T(8,128)(2,1)}, bf16[2,144,2048]{2,1,0:T(8,128)(2,1)}, u32[]{:S(2)}, u32[]{:S(2)}) collective-permute-start(bf16[2,144,2048]{2,1,0:T(8,128)(2,1)} %get-tuple-element.63), channel_id=1, source_target_pairs={{0,1},{1,0},{2,3},{3,2},{4,5},{5,4},{6,7},{7,6},{8,9},{9,8},{10,11... | collective-permute-start | bytes 3538952 | tf_op jit(solution)/shard_map/ppermute | solution.py:382
  283.9 22.3 %collective-permute-start.27 = (bf16[2,512,512]{2,1,0:T(8,128)(2,1)}, bf16[2,512,512]{2,1,0:T(8,128)(2,1)}, u32[]{:S(2)}, u32[]{:S(2)}) collective-permute-start(bf16[2,512,512]{2,1,0:T(8,128)(2,1)} %get-tuple-element.69), channel_id=1, source_target_pairs={{0,1},{1,0},{2,3},{3,2},{4,5},{5,4},{6,7},{7,6},{8,9},{9,8},{10,11... | collective-permute-start | bytes 3145736 | tf_op jit(solution)/shard_map/ppermute | solution.py:382
  287.2 23.4 %collective-permute-start.26 = (bf16[128,2048]{1,0:T(8,128)(2,1)}, bf16[128,2048]{1,0:T(8,128)(2,1)}, u32[]{:S(2)}, u32[]{:S(2)}) collective-permute-start(bf16[128,2048]{1,0:T(8,128)(2,1)} %slice_bitcast_fusion.4), channel_id=1, source_target_pairs={{0,2},{1,3},{2,0},{3,1},{4,6},{5,7},{6,4},{7,5},{8,10},{9,11},{10,... | collective-permute-start | bytes 1572872 | tf_op jit(solution)/shard_map/ppermute | solution.py:382
  341.9 19.7 %collective-permute-start.32 = (bf16[1024,512]{1,0:T(8,128)(2,1)}, bf16[1024,512]{1,0:T(8,128)(2,1)}, u32[]{:S(2)}, u32[]{:S(2)}) collective-permute-start(bf16[1024,512]{1,0:T(8,128)(2,1)} %constant_dynamic-slice_fusion), channel_id=1, source_target_pairs={{0,1},{1,0},{2,3},{3,2},{4,5},{5,4},{6,7},{7,6},{8,9},{9,8},{10,11... | collective-permute-start | bytes 3145736 | tf_op jit(solution)/shard_map/ppermute | solution.py:382
  354.2 23.2 %all-to-all-start.4 = ((bf16[8,18,2048]{2,1,0:T(8,128)(2,1)}), bf16[8,18,2048]{2,1,0:T(8,128)(2,1)S(1)}, u32[]{:S(2)}, u32[]{:S(2)}) async-start(bf16[8,18,2048]{2,1,0:T(8,128)(2,1)} %reshape.306), calls=%async_computation.4 | async-start | bytes 1572864 | tf_op jit(solution)/shard_map/all_to_all | solution.py:398
  359.8 26.3 %collective-permute-start.30 = (bf16[256,2048]{1,0:T(8,128)(2,1)S(1)}, bf16[256,2048]{1,0:T(8,128)(2,1)}, u32[]{:S(2)}, u32[]{:S(2)}) collective-permute-start(bf16[256,2048]{1,0:T(8,128)(2,1)S(1)} %add_convert_fusion.4), channel_id=1, source_target_pairs={{0,2},{1,3},{2,0},{3,1},{4,6},{5,7},{6,4},{7,5},{8,10},{9,11},{10,... | collective-permute-start | bytes 3145736 | tf_op jit(solution)/shard_map/ppermute | solution.py:382
  363.4 43.0 %collective-permute-start.33 = (bf16[1024,512]{1,0:T(8,128)(2,1)S(1)}, bf16[1024,512]{1,0:T(8,128)(2,1)}, u32[]{:S(2)}, u32[]{:S(2)}) collective-permute-start(bf16[1024,512]{1,0:T(8,128)(2,1)S(1)} %add_convert_fusion.2), channel_id=1, source_target_pairs={{0,2},{1,3},{2,0},{3,1},{4,6},{5,7},{6,4},{7,5},{8,10},{9,11},{10,... | collective-permute-start | bytes 3145736 | tf_op jit(solution)/shard_map/ppermute | solution.py:382
  387.7 35.5 %collective-permute-start.31 = (bf16[256,2048]{1,0:T(8,128)(2,1)S(1)}, bf16[256,2048]{1,0:T(8,128)(2,1)}, u32[]{:S(2)}, u32[]{:S(2)}) collective-permute-start(bf16[256,2048]{1,0:T(8,128)(2,1)S(1)} %add_convert_fusion.3), channel_id=1, source_target_pairs={{0,1},{1,0},{2,3},{3,2},{4,5},{5,4},{6,7},{7,6},{8,9},{9,8},{10,11... | collective-permute-start | bytes 3145736 | tf_op jit(solution)/shard_map/ppermute | solution.py:382
  417.5 20.8 %all-to-all-start.9 = ((bf16[8,16,2048]{2,1,0:T(8,128)(2,1)}), bf16[8,16,2048]{2,1,0:T(8,128)(2,1)S(1)}, u32[]{:S(2)}, u32[]{:S(2)}) async-start(bf16[8,16,2048]{2,1,0:T(8,128)(2,1)} %broadcast_in_dim.48), calls=%async_computation.9 | async-start | bytes 1048576 | tf_op jit(solution)/shard_map/all_to_all | solution.py:400
  439.3 24.0 %all-to-all-start.5 = ((bf16[8,18,2048]{2,1,0:T(8,128)(2,1)}), bf16[8,18,2048]{2,1,0:T(8,128)(2,1)S(1)}, u32[]{:S(2)}, u32[]{:S(2)}) async-start(bf16[8,18,2048]{2,1,0:T(8,128)(2,1)} %broadcast_in_dim.46), calls=%async_computation.5 | async-start | bytes 1572864 | tf_op jit(solution)/shard_map/all_to_all | solution.py:400
  (55 other events, 859.9 us)
